TPU v7x, 32 devices: a whole 2x2x4 slice. The times are simulated.
32 devices in a mesh: seq: 8 (over z, x), grp: 4 (over y, core).
Axes of the slice: x: 2, y: 2, z: 4, core: 2. Of those that a mesh axis runs over, the one named last changes fastest.
Arguments:
- in_gate: bfloat16 [8192, 512], P(('grp', 'seq')), parts along dimension 0, may hold values from -6 to 6
- values: bfloat16 [8192, 512], P(('grp', 'seq')), parts along dimension 0, may hold values from -6 to 6
- out_gate: bfloat16 [8192, 512], P(('grp', 'seq')), parts along dimension 0, may hold values from -6 to 6
- filter_taps: bfloat16 [2048, 512], P('seq'), may hold values from -0.125 to 0.125
- skip_gain: float32 [512], replicated, may hold values from -4 to 4
Outputs:
- mixed: bfloat16 [8192, 512], P(('grp', 'seq')), parts along dimension 0
There are 4 independent parts, one for each index of `grp`. A program takes and returns all parts, laid end to end along the dimension named above; an argument that names none is the same for every part. Nothing has to cross between parts.
All inputs are finite; a program needn't handle non-finite values.
Results may differ from a plain program's by a relative error of at most 0.001.
Values sent between devices are 32-bit elements; how exact they have to be, the bound alone decides.
A program may use at most 64 MiB of HBM per device.

v0:
```python
import jax
import jax.numpy as jnp
from jax import lax
from jax.sharding import PartitionSpec as P

exact_mode = lax.Precision.HIGHEST


def tables(count):
    index_row = jnp.arange(count, dtype=jnp.int32)
    product = index_row[:, None] * index_row[None, :] % count
    angles = product.astype(jnp.float32) * (2.0 * jnp.pi / count)
    return (jnp.cos(angles), jnp.sin(angles))


def transform(cosine_table, sine_table, real_part, imag_part, pattern, inverse):
    cos_real = jnp.einsum(pattern, cosine_table, real_part, precision=exact_mode)
    cos_imag = jnp.einsum(pattern, cosine_table, imag_part, precision=exact_mode)
    sin_real = jnp.einsum(pattern, sine_table, real_part, precision=exact_mode)
    sin_imag = jnp.einsum(pattern, sine_table, imag_part, precision=exact_mode)
    if inverse:
        return (cos_real - sin_imag, cos_imag + sin_real)
    return (cos_real + sin_imag, cos_imag - sin_real)


def rotate(real_part, imag_part, angles, inverse):
    cosine = jnp.cos(angles)
    sine_part = jnp.sin(angles)
    if inverse:
        return (
            real_part * cosine - imag_part * sine_part,
            imag_part * cosine + real_part * sine_part,
        )
    return (real_part * cosine + imag_part * sine_part, imag_part * cosine - real_part * sine_part)


def local(in_gate, values, out_gate, filter_taps, skip_gain):
    own_rows, channels = in_gate.shape
    devices = lax.axis_size("seq")
    own_index = lax.axis_index("seq")
    seq_total = own_rows * devices
    group_rows = own_rows // devices
    gated = in_gate.astype(jnp.float32) * values.astype(jnp.float32)
    taps_real = filter_taps.astype(jnp.float32)
    cos_small, sin_small = tables(devices)
    cos_large, sin_large = tables(own_rows)
    halves = jnp.arange(2, dtype=jnp.float32)
    half_scale = jnp.pi / seq_total
    position = own_index * own_rows + jnp.arange(own_rows, dtype=jnp.int32)
    phases = halves[:, None] * position.astype(jnp.float32)[None, :] * half_scale
    signals = jnp.stack([gated, taps_real])
    real_part = signals[:, None] * jnp.cos(phases)[None, :, :, None]
    imag_part = -signals[:, None] * jnp.sin(phases)[None, :, :, None]
    packed = jnp.stack([real_part, imag_part]).reshape(8, 1, own_rows, channels)
    arrived = lax.all_to_all(packed, "seq", split_axis=2, concat_axis=1, tiled=True)
    arrived = arrived.reshape(2, 4, devices, group_rows, channels)
    real_part = arrived[0]
    imag_part = arrived[1]
    real_part, imag_part = transform(
        cos_small, sin_small, real_part, imag_part, "ap,gpsc->gasc", False
    )
    local_pos = own_index * group_rows + jnp.arange(group_rows, dtype=jnp.int32)
    twist_index = jnp.arange(devices, dtype=jnp.int32)[:, None] * local_pos[None, :] % seq_total
    twist_angles = (twist_index.astype(jnp.float32) * (2.0 * jnp.pi / seq_total))[None, :, :, None]
    real_part, imag_part = rotate(real_part, imag_part, twist_angles, False)
    packed = jnp.stack([real_part, imag_part])[:, :, :, None]
    arrived = lax.all_to_all(packed, "seq", split_axis=2, concat_axis=3, tiled=True)
    arrived = arrived.reshape(2, 4, own_rows, channels)
    real_part, imag_part = transform(
        cos_large, sin_large, arrived[0], arrived[1], "br,grc->gbc", False
    )
    data_real = real_part[0:2]
    data_imag = imag_part[0:2]
    taps_re = real_part[2:4]
    taps_im = imag_part[2:4]
    prod_real = data_real * taps_re - data_imag * taps_im
    prod_imag = data_real * taps_im + data_imag * taps_re
    real_part, imag_part = transform(
        cos_large, sin_large, prod_real, prod_imag, "rb,gbc->grc", True
    )
    back_index = own_index * jnp.arange(own_rows, dtype=jnp.int32) % seq_total
    back_angles = (back_index.astype(jnp.float32) * (2.0 * jnp.pi / seq_total))[None, :, None]
    real_part, imag_part = rotate(real_part, imag_part, back_angles, True)
    packed = jnp.stack([real_part, imag_part]).reshape(2, 2, 1, devices, group_rows, channels)
    arrived = lax.all_to_all(packed, "seq", split_axis=3, concat_axis=2, tiled=True)
    arrived = arrived.reshape(2, 2, devices, group_rows, channels)
    real_part, imag_part = transform(
        cos_small, sin_small, arrived[0], arrived[1], "pa,gasc->gpsc", True
    )
    norm_factor = 1.0 / (2.0 * seq_total)
    packed = jnp.stack([real_part, imag_part])[:, :, :, None]
    arrived = lax.all_to_all(packed, "seq", split_axis=2, concat_axis=3, tiled=True)
    arrived = arrived.reshape(2, 2, own_rows, channels)
    position = own_index * own_rows + jnp.arange(own_rows, dtype=jnp.int32)
    phases = (halves[:, None] * position.astype(jnp.float32)[None, :] * half_scale)[:, :, None]
    conv = (
        jnp.sum(arrived[0] * jnp.cos(phases) - arrived[1] * jnp.sin(phases), axis=0) * norm_factor
    )
    total = conv + skip_gain[None, :] * gated
    return (out_gate.astype(jnp.float32) * total).astype(jnp.bfloat16)


def solution(mesh):
    in_specs = (
        P(("grp", "seq"), None),
        P(("grp", "seq"), None),
        P(("grp", "seq"), None),
        P("seq", None),
        P(),
    )
    out_specs = P(("grp", "seq"), None)
    return jax.shard_map(local, mesh=mesh, in_specs=in_specs, out_specs=out_specs, check_vma=False)
```

profile of v0, /device:TPU:0, one launch (start us, length us, event | category | flops | bytes accessed | tf_op | source)
XLA Modules:
  0.0 385.4 jit_solution(5581030762943034759)
XLA Ops:
  0.0 0.1 fusion.90
  0.1 0.1 copy.80
  0.2 0.1 copy.82
  0.4 1.0 bitcast_convert_fusion
  1.4 1.1 fusion.26
  2.5 0.2 pad_maximum_fusion.2
  2.7 0.8 copy.79
  3.6 0.8 copy.81
  4.4 2.1 broadcast_multiply_fusion
  6.5 4.1 %pad_maximum_fusion = f32[2,2,2,256,512]{4,2,1,0,3:T(2,128)} fusion(f32[1,2,2,256,512]{4,2,1,0,3:T(2,128)S(1)} %get-tuple-element.27, f32[1,2,2,256,512]{4,2,1,0,3:T(2,128)S(1)} %get-tuple-element.28), kind=kLoop, calls=%fused_computation | loop fusion | flops 1048576 | bytes 8388608 | tf_op jit(solution)/shard_map/stack | solution.py:54
  10.6 6.1 %reshape.276 = f32[8,1,256,512]{3,0,1,2:T(8,128)} reshape(f32[2,2,2,256,512]{4,2,1,0,3:T(2,128)} %pad_maximum_fusion) | data formatting | bytes 8388608 | tf_op jit(solution)/shard_map/reshape | solution.py:54
  16.7 7.7 %all-to-all-start = ((f32[8,1,256,512]{3,0,1,2:T(8,128)}), f32[8,1,256,512]{3,0,1,2:T(8,128)}, u32[]{:S(2)}, u32[]{:S(2)}) async-start(f32[8,1,256,512]{3,0,1,2:T(8,128)} %reshape.276), calls=%async_computation | async-start | bytes 8388608 | tf_op jit(solution)/shard_map/all_to_all | solution.py:55
  24.4 0.2 fusion.64
  24.5 92.7 %all-to-all-done = f32[8,1,256,512]{3,0,1,2:T(8,128)} async-done(((f32[8,1,256,512]{3,0,1,2:T(8,128)}), f32[8,1,256,512]{3,0,1,2:T(8,128)}, u32[]{:S(2)}, u32[]{:S(2)}) %all-to-all-start) | async-done | bytes 4194336 | tf_op jit(solution)/shard_map/all_to_all | solution.py:55
  117.2 4.5 %fusion.162 = (f32[4,1,256,512]{3,0,1,2:T(4,128)S(1)}, f32[4,1,256,512]{3,0,1,2:T(4,128)S(1)}) fusion(f32[8,1,256,512]{3,0,1,2:T(8,128)} %all-to-all-done), kind=kLoop, calls=%fused_computation.188 | loop fusion | bytes 8388608 | tf_op jit(solution)/shard_map/slice | solution.py:57
  121.7 0.7 copy.120
  122.4 3.2 fusion.6
  125.6 3.2 fusion.4
  128.8 0.7 copy.119
  129.5 3.6 fusion.12
  133.1 3.9 %fusion.1 = (f32[1,4,8,32,512]{4,2,3,1,0:T(8,128)S(1)}, f32[1,4,8,32,512]{4,2,3,1,0:T(8,128)S(1)}) fusion(f32[4,32,512,8]{2,3,1,0:T(8,128)S(1)} %fusion.12, f32[8,32]{0,1:T(8,128)S(1)} %get-tuple-element.24, f32[8,32]{0,1:T(8,128)S(1)} %get-tuple-element.23, f32[4,32,512,8]{2,3,1,0:T(8,128)S(1)} %fusion.4, f32[4,8,32,512]{3,2,1,0:T(8,128)S(1)} %bitcast.122), kind=kOutput, calls=%fused_computation.7 | convolution fusion | flops 54002560 | bytes 10487808 | tf_op jit(solution)/shard_map/ap,gpsc->gasc/dot_general | solution.py:19
  137.0 0.4 maximum_bitcast_fusion
  137.5 4.4 %copy.89 = f32[2,4,8,1,32,512]{5,4,1,0,3,2:T(8,128)} copy(f32[2,4,8,1,32,512]{5,2,4,1,0,3:T(8,128)S(1)} %maximum_bitcast_fusion) | data formatting | bytes 8388608 | tf_op jit(solution)/shard_map/broadcast_in_dim | solution.py:66
  141.9 4.8 %all-to-all-start.1 = ((f32[2,4,8,1,32,512]{5,4,1,0,3,2:T(8,128)}), f32[2,4,8,1,32,512]{5,4,1,0,3,2:T(8,128)}, u32[]{:S(2)}, u32[]{:S(2)}) async-start(f32[2,4,8,1,32,512]{5,4,1,0,3,2:T(8,128)} %copy.89), calls=%async_computation.1 | async-start | bytes 8388608 | tf_op jit(solution)/shard_map/all_to_all | solution.py:67
  146.7 0.1 fusion.94
  146.7 92.3 %all-to-all-done.1 = f32[2,4,8,1,32,512]{5,4,1,0,3,2:T(8,128)} async-done(((f32[2,4,8,1,32,512]{5,4,1,0,3,2:T(8,128)}), f32[2,4,8,1,32,512]{5,4,1,0,3,2:T(8,128)}, u32[]{:S(2)}, u32[]{:S(2)}) %all-to-all-start.1) | async-done | bytes 4194336 | tf_op jit(solution)/shard_map/all_to_all | solution.py:67
  239.0 2.7 fusion.161
  241.7 0.2 copy.121
  242.0 4.4 %fusion.40 = f32[4,512,256]{2,1,0:T(8,128)S(1)} fusion(f32[4,256,512]{2,1,0:T(8,128)S(1)} %bitcast.123), kind=kOutput, calls=%fused_computation.68 | convolution fusion | flops 1611530240 | bytes 4194304 | tf_op jit(solution)/shard_map/br,grc->gbc/dot_general | solution.py:17
  246.4 0.2 copy.122
  246.7 4.4 %fusion.38 = f32[4,512,256]{2,1,0:T(8,128)S(1)} fusion(f32[4,256,512]{2,1,0:T(8,128)S(1)} %bitcast.125), kind=kOutput, calls=%fused_computation.66 | convolution fusion | flops 1611530240 | bytes 4194304 | tf_op jit(solution)/shard_map/br,grc->gbc/dot_general | solution.py:18
  251.1 4.9 %add_bitcast_fusion = f32[4,256,512]{1,2,0:T(8,128)S(1)} fusion(f32[4,512,256]{2,1,0:T(8,128)S(1)} %fusion.40, f32[4,256,512]{2,1,0:T(8,128)S(1)} %bitcast.126), kind=kOutput, calls=%fused_computation.13 | convolution fusion | flops 1612054528 | bytes 6291456 | tf_op jit(solution)/shard_map/br,grc->gbc/dot_general | solution.py:20
  256.0 4.5 %subtract_bitcast_fusion = f32[4,256,512]{1,2,0:T(8,128)S(1)} fusion(f32[4,512,256]{2,1,0:T(8,128)S(1)} %fusion.38, f32[4,256,512]{2,1,0:T(8,128)S(1)} %bitcast.124), kind=kOutput, calls=%fused_computation.12 | convolution fusion | flops 1612054528 | bytes 6291456 | tf_op jit(solution)/shard_map/br,grc->gbc/dot_general | solution.py:19
  260.5 0.3 multiply_add_fusion.1
  260.8 2.1 fusion.36
  262.9 2.1 fusion.34
  265.0 2.3 convolution_subtract_fusion.1
  267.2 2.3 multiply_subtract_fusion
  269.6 0.3 pad_maximum_fusion.1
  269.8 0.3 copy.117
  270.1 51.8 %all_to_all.16 = f32[2,2,1,8,32,512]{5,4,1,2,0,3:T(8,128)S(1)} all-to-all(f32[2,2,1,8,32,512]{5,4,1,2,0,3:T(8,128)S(1)} %copy.117), channel_id=1, replica_groups=mesh['seq'=8,'grp'=4] {'seq'}, dimensions={3} | all-to-all | bytes 4194304 | tf_op jit(solution)/shard_map/all_to_all | solution.py:85
  321.9 0.3 fusion.163
  322.2 1.6 fusion.22
  323.8 1.6 fusion.23
  325.5 1.7 fusion.19
  327.2 1.7 fusion.18
  329.0 0.2 maximum_bitcast_fusion.1
  329.2 2.6 copy.104
  331.7 3.6 all-to-all-start.3
  335.4 0.1 fusion.62
  335.5 47.7 %all-to-all-done.3 = f32[2,2,8,1,32,512]{5,4,1,0,3,2:T(8,128)S(1)} async-done(((f32[2,2,8,1,32,512]{5,4,1,0,3,2:T(8,128)}), f32[2,2,8,1,32,512]{5,4,1,0,3,2:T(8,128)S(1)}, u32[]{:S(2)}, u32[]{:S(2)}) %all-to-all-start.3) | async-done | bytes 2097184 | tf_op jit(solution)/shard_map/all_to_all | solution.py:92
  383.2 0.0 copy-start
  383.2 0.0 copy-start.1
  383.2 0.0 copy-start.2
  383.2 0.0 copy-start.3
  383.3 0.2 fusion.21
  383.5 0.3 copy_multiply_fusion
  383.8 0.3 copy.106
  384.1 0.1 copy-done
  384.2 0.1 copy-done.1
  384.3 0.1 copy-done.2
  384.4 0.0 copy-done.3
  384.4 0.9 fusion.25
  (3 shorter events, 0.0 us)
Async XLA Ops:
  16.7 100.5 %all-to-all-start = ((f32[8,1,256,512]{3,0,1,2:T(8,128)}), f32[8,1,256,512]{3,0,1,2:T(8,128)}, u32[]{:S(2)}, u32[]{:S(2)}) async-start(f32[8,1,256,512]{3,0,1,2:T(8,128)} %reshape.276), calls=%async_computation | async-start | bytes 8388608 | tf_op jit(solution)/shard_map/all_to_all | solution.py:55
  141.9 97.1 %all-to-all-start.1 = ((f32[2,4,8,1,32,512]{5,4,1,0,3,2:T(8,128)}), f32[2,4,8,1,32,512]{5,4,1,0,3,2:T(8,128)}, u32[]{:S(2)}, u32[]{:S(2)}) async-start(f32[2,4,8,1,32,512]{5,4,1,0,3,2:T(8,128)} %copy.89), calls=%async_computation.1 | async-start | bytes 8388608 | tf_op jit(solution)/shard_map/all_to_all | solution.py:67
  331.7 51.5 %all-to-all-start.3 = ((f32[2,2,8,1,32,512]{5,4,1,0,3,2:T(8,128)}), f32[2,2,8,1,32,512]{5,4,1,0,3,2:T(8,128)S(1)}, u32[]{:S(2)}, u32[]{:S(2)}) async-start(f32[2,2,8,1,32,512]{5,4,1,0,3,2:T(8,128)} %copy.104), calls=%async_computation.3 | async-start | bytes 4194304 | tf_op jit(solution)/shard_map/all_to_all | solution.py:92
  383.2 1.0 copy-start
  383.2 1.0 copy-start.1
  383.2 1.1 copy-start.2
  383.2 1.1 copy-start.3
where the time goes:
time: 390 us; the launch traced here: 385 us
  waiting for transfers between devices  233 us (60%)
  blocking collectives  51.8 us (13%)
  matrix products  47.7 us (12%)
  local copies, waits for them, and re-layouts  25.1 us (6%)
  starting transfers between devices  16.1 us (4%)
  other arithmetic  11.6 us (3%)
    all_to_all x2, waiting for transfers between devices, local(): lax.all_to_all(packed, 'seq', split_axis=2, concat_axis=3, tiled=True)  140 us
    all_to_all x1, waiting for transfers between devices, local(): lax.all_to_all(packed, 'seq', split_axis=2, concat_axis=1, tiled=True)  92.7 us
    all_to_all x1, blocking collectives, local(): lax.all_to_all(packed, 'seq', split_axis=3, concat_axis=2, tiled=True)  51.8 us
    dot_general x4, matrix products, transform(): sin_real = jnp.einsum(pattern, sine_table, real_part, precision=exact_mode)  12.4 us
    dot_general x4, matrix products, transform(): sin_imag = jnp.einsum(pattern, sine_table, imag_part, precision=exact_mode)  12.1 us
    dot_general x4, matrix products, transform(): jnp.einsum(pattern, cosine_table, real_part, precision=exact_mode)  11.7 us
    dot_general x4, matrix products, transform(): jnp.einsum(pattern, cosine_table, imag_part, precision=exact_mode)  11.4 us
    all_to_all x2, starting transfers between devices, local(): lax.all_to_all(packed, 'seq', split_axis=2, concat_axis=3, tiled=True)  8.41 us
  transfers between devices with their start and end apart: 3, of which 3 were waited for; matrix products, arithmetic and copies ran while one was open for 0% of the time, Pallas kernels for 0%

commit v1 on v0

v1 whole, which is shorter than its diff:
```python
import functools

import jax
import jax.numpy as jnp
from jax import lax
from jax.experimental import pallas as pl
from jax.experimental.pallas import tpu as pltpu
from jax.sharding import PartitionSpec as P

LANES = 128
COARSE = 16
FINE = 8
CHUNK = 16


def kernel(
    devices,
    in_gate,
    values,
    out_gate,
    taps,
    skip_gain,
    mixed,
    sent,
    held,
    block,
    turned,
    back,
    conv,
    send_sem,
    recv_sem,
    back_send_sem,
    back_recv_sem,
):
    own, channels = in_gate.shape
    share = channels // devices
    chunks = share // CHUNK
    per_owner = own // LANES
    count = per_owner * devices
    width = FINE * count
    me = lax.axis_index("seq")

    barrier = pltpu.get_barrier_semaphore()
    for step in range(1, devices):
        peer = lax.rem(me + step, devices)
        pl.semaphore_signal(
            barrier, inc=1, device_id={"seq": peer}, device_id_type=pl.DeviceIdType.MESH
        )

    flip = (
        lax.broadcasted_iota(jnp.int32, (own, own), 0)
        + lax.broadcasted_iota(jnp.int32, (own, own), 1)
        == own - 1
    )
    flip = flip.astype(jnp.float32).astype(jnp.bfloat16)
    taps_turned = taps[...].astype(jnp.float32).T.astype(jnp.bfloat16)
    taps_turned = jnp.dot(taps_turned, flip, preferred_element_type=jnp.float32)
    gated = in_gate[...].astype(jnp.float32) * values[...].astype(jnp.float32)
    gated = gated.T
    for u in range(per_owner):
        sent[0, u] = gated[:, u * LANES : (u + 1) * LANES]
        sent[1, u] = taps_turned[:, u * LANES : (u + 1) * LANES]

    pl.semaphore_wait(barrier, devices - 1)

    def rows_of(device, chunk):
        return pl.ds(pl.multiple_of(device * share + chunk * CHUNK, CHUNK), CHUNK)

    def forward(step, chunk):
        peer = lax.rem(me + step, devices)
        return pltpu.make_async_remote_copy(
            src_ref=sent.at[:, :, rows_of(peer, chunk), :],
            dst_ref=held.at[me, :, :, pl.ds(chunk * CHUNK, CHUNK), :],
            send_sem=send_sem.at[step, chunk],
            recv_sem=recv_sem.at[step, chunk],
            device_id={"seq": peer},
            device_id_type=pl.DeviceIdType.MESH,
        )

    def backward(step, chunk):
        peer = lax.rem(me + step, devices)
        return pltpu.make_async_remote_copy(
            src_ref=turned.at[chunk, owner_rows(peer), :],
            dst_ref=back.at[me * chunks + chunk],
            send_sem=back_send_sem.at[step, chunk],
            recv_sem=back_recv_sem.at[step, chunk],
            device_id={"seq": peer},
            device_id_type=pl.DeviceIdType.MESH,
        )

    def owner_rows(device):
        start = FINE * per_owner * (devices - 1 - device)
        return pl.ds(pl.multiple_of(start, FINE * per_owner), FINE * per_owner)

    for chunk in range(chunks):
        for step in range(1, devices):
            forward(step, chunk).start()
    for chunk in range(chunks):
        rows = slice(chunk * CHUNK, (chunk + 1) * CHUNK)
        held[me, :, :, rows, :] = sent[:, :, rows_of(me, chunk), :]

    coarse_row = lax.broadcasted_iota(jnp.int32, (COARSE, LANES), 0)
    coarse_lane = lax.broadcasted_iota(jnp.int32, (COARSE, LANES), 1)
    coarse_mask = coarse_lane >= FINE * coarse_row
    fine_row = lax.broadcasted_iota(jnp.int32, (FINE, LANES), 0)
    fine_lane = lax.broadcasted_iota(jnp.int32, (FINE, LANES), 1)
    fine_mask = fine_lane + (FINE - 1) - fine_row < LANES
    wide_lane = lax.broadcasted_iota(jnp.int32, (COARSE, width), 1)

    def convolve(chunk, at, carry):
        row = pl.ds(chunk * CHUNK + at, 1)
        pieces = []
        before = jnp.zeros((COARSE, LANES), jnp.float32)
        for m in range(count):
            line = held[m // per_owner, 0, m % per_owner, row, :]
            rolled = pltpu.roll(
                jnp.broadcast_to(line, (COARSE, LANES)), 0, 1, stride=FINE, stride_axis=0
            )
            shifted = jnp.where(coarse_mask, rolled, before)
            before = rolled
            high = shifted.astype(jnp.bfloat16)
            low = (shifted - high.astype(jnp.float32)).astype(jnp.bfloat16)
            pieces.append(jnp.concatenate([high, low], axis=1))
        signal = jnp.concatenate(pieces, axis=0)
        pieces = []
        after = jnp.zeros((FINE, LANES), jnp.float32)
        for b in range(count - 1, -1, -1):
            line = held[devices - 1 - b // per_owner, 1, b % per_owner, row, :]
            rolled = pltpu.roll(
                jnp.broadcast_to(line, (FINE, LANES)),
                LANES - FINE + 1,
                1,
                stride=1,
                stride_axis=0,
            )
            pieces.append(jnp.where(fine_mask, rolled, after))
            after = rolled
        filters = jnp.concatenate(pieces[::-1], axis=0).astype(jnp.bfloat16)
        filters = jnp.concatenate([filters, filters], axis=1)
        product = lax.dot_general(
            signal, filters, (((1,), (1,)), ((), ())), preferred_element_type=jnp.float32
        )
        total = product[0:COARSE]
        for m in range(1, count):
            part = product[m * COARSE : (m + 1) * COARSE]
            part = jnp.where(wide_lane >= FINE * m, part, 0.0)
            total = total + pltpu.roll(part, width - FINE * m, 1)
        for group in range(width // LANES):
            block[group, pl.ds(at, COARSE, stride=CHUNK), :] = total[
                :, group * LANES : (group + 1) * LANES
            ]
        return carry

    for chunk in range(chunks):
        for step in range(1, devices):
            forward(step, chunk).wait_recv()
        lax.fori_loop(0, CHUNK, functools.partial(convolve, chunk), 0)
        for group in range(width // LANES):
            turned[chunk, group * LANES : (group + 1) * LANES, :] = block[group].T
        for step in range(1, devices):
            backward(step, chunk).start()
        back[me * chunks + chunk] = turned[chunk, owner_rows(me), :]

    for chunk in range(chunks):
        for step in range(1, devices):
            forward(step, chunk).wait_send()
            backward(step, chunk).wait_send()
            backward(step, chunk).wait_recv()

    parts = LANES // CHUNK

    def place(group, carry):
        for a in range(COARSE):
            lanes = pl.ds(a * CHUNK, CHUNK)
            merged = jnp.concatenate(
                [back[group * parts + part, :, lanes] for part in range(parts)], axis=1
            )
            for u in range(per_owner):
                start = LANES * (per_owner - 1 - u) + FINE * (COARSE - 1 - a)
                conv[group, start : start + FINE, :] = merged[u * FINE : (u + 1) * FINE]
        return carry

    lax.fori_loop(0, channels // LANES, place, 0)
    for group in range(channels // LANES):
        lanes = slice(group * LANES, (group + 1) * LANES)
        gated = in_gate[:, lanes].astype(jnp.float32) * values[:, lanes].astype(jnp.float32)
        total = conv[group] + skip_gain[:, lanes] * gated
        mixed[:, lanes] = (out_gate[:, lanes].astype(jnp.float32) * total).astype(jnp.bfloat16)


def local(in_gate, values, out_gate, filter_taps, skip_gain):
    own, channels = in_gate.shape
    devices = lax.axis_size("seq")
    share = channels // devices
    chunks = share // CHUNK
    width = FINE * (own // LANES) * devices
    owned = FINE * (own // LANES)
    vmem = pl.BlockSpec(memory_space=pltpu.VMEM)
    return pl.pallas_call(
        functools.partial(kernel, devices),
        out_shape=jax.ShapeDtypeStruct((own, channels), jnp.bfloat16),
        in_specs=[vmem] * 5,
        out_specs=vmem,
        scratch_shapes=[
            pltpu.VMEM((2, own // LANES, channels, LANES), jnp.float32),
            pltpu.VMEM((devices, 2, own // LANES, share, LANES), jnp.float32),
            pltpu.VMEM((width // LANES, COARSE * CHUNK, LANES), jnp.float32),
            pltpu.VMEM((chunks, width, COARSE * CHUNK), jnp.float32),
            pltpu.VMEM((devices * chunks, owned, COARSE * CHUNK), jnp.float32),
            pltpu.VMEM((channels // LANES, own, LANES), jnp.float32),
            pltpu.SemaphoreType.DMA((devices, chunks)),
            pltpu.SemaphoreType.DMA((devices, chunks)),
            pltpu.SemaphoreType.DMA((devices, chunks)),
            pltpu.SemaphoreType.DMA((devices, chunks)),
        ],
        compiler_params=pltpu.CompilerParams(
            collective_id=0, has_side_effects=True, vmem_limit_bytes=40 * 1024 * 1024
        ),
    )(in_gate, values, out_gate, filter_taps, skip_gain.reshape(1, channels))


def solution(mesh):
    in_specs = (
        P(("grp", "seq"), None),
        P(("grp", "seq"), None),
        P(("grp", "seq"), None),
        P("seq", None),
        P(),
    )
    out_specs = P(("grp", "seq"), None)
    return jax.shard_map(local, mesh=mesh, in_specs=in_specs, out_specs=out_specs, check_vma=False)
```

time: 390 us -> 54.7 us (0.14); the launches traced: 385 us -> 54.4 us
  waiting for transfers between devices: 233 us -> 0 us
  blocking collectives: 51.8 us -> 0 us
  Pallas kernels: 0 us -> 49.2 us
  matrix products: 47.7 us -> 0 us
  local copies, waits for them, and re-layouts: 25.1 us -> 5.18 us
  starting transfers between devices: 16.1 us -> 0 us
  other arithmetic: 11.6 us -> 0 us
    all_to_all x3 -> x0, waiting for transfers between devices: 233 us -> none  [the longest x2 140 us: local(): lax.all_to_all(packed, 'seq', split_axis=2, concat_axis=3, tiled=True)]
    all_to_all x1 -> x0, blocking collectives: 51.8 us -> none  [local(): lax.all_to_all(packed, 'seq', split_axis=3, concat_axis=2, tiled=True)]
    pallas_call x0 -> x1, Pallas kernels: none -> 49.2 us  [local(): pl.pallas_call(functools.partial(kernel, devices), out_shape=jax.ShapeDty...]
    dot_general x16 -> x0, matrix products: 47.7 us -> none  [the longest x4 12.4 us: transform(): sin_real = jnp.einsum(pattern, sine_table, real_part, precision=exact_mode)]
    all_to_all x3 -> x0, starting transfers between devices: 16.1 us -> none  [the longest x2 8.41 us: local(): lax.all_to_all(packed, 'seq', split_axis=2, concat_axis=3, tiled=True)]
    slice x3 -> x0, local copies, waits for them, and re-layouts: 7.51 us -> none  [the longest x1 4.52 us: local(): real_part = arrived[0]]
    broadcast_in_dim x2 -> x0, local copies, waits for them, and re-layouts: 6.97 us -> none  [local(): packed = jnp.stack([real_part, imag_part])[:, :, :, None]]
    another operation x5 -> x0, other arithmetic: 6.71 us -> none  [the longest x1 4.1 us: local(): packed = jnp.stack([real_part, imag_part]).reshape(8, 1, own_rows, channels)]
  transfers between devices with their start and end apart: 3 -> 0, of which waited for: 3 -> 0; matrix products, arithmetic and copies ran while one was open for 0% -> 0% of each run, Pallas kernels for 0% -> 0%
where the time goes in v1:
time: 54.7 us; the launch traced here: 54.4 us
  Pallas kernels  49.2 us (90%)
  local copies, waits for them, and re-layouts  5.18 us (9%)
    pallas_call x1, Pallas kernels, local(): pl.pallas_call(functools.partial(kernel, devices), out_shape=jax.ShapeDty...  49.2 us
    unnamed x11, local copies, waits for them, and re-layouts  5.18 us

profile of v1, /device:TPU:0, one launch (start us, length us, event | category | flops | bytes accessed | tf_op | source)
XLA Modules:
  0.0 54.4 jit_solution(6934928901090900808)
XLA Ops:
  0.0 0.0 copy-start
  0.0 0.9 %copy-done = bf16[256,512]{1,0:T(8,128)(2,1)S(1)} copy-done((bf16[256,512]{1,0:T(8,128)(2,1)S(1)}, bf16[256,512]{1,0:T(8,128)(2,1)}, u32[]{:S(2)}) %copy-start) | copy-done | bytes 262168
  1.0 0.0 copy-start.1
  1.0 0.9 %copy-done.1 = bf16[256,512]{1,0:T(8,128)(2,1)S(1)} copy-done((bf16[256,512]{1,0:T(8,128)(2,1)S(1)}, bf16[256,512]{1,0:T(8,128)(2,1)}, u32[]{:S(2)}) %copy-start.1) | copy-done | bytes 262168
  1.9 0.0 copy-start.2
  1.9 0.9 %copy-done.2 = bf16[256,512]{1,0:T(8,128)(2,1)S(1)} copy-done((bf16[256,512]{1,0:T(8,128)(2,1)S(1)}, bf16[256,512]{1,0:T(8,128)(2,1)}, u32[]{:S(2)}) %copy-start.2) | copy-done | bytes 262168
  2.9 0.0 copy-start.3
  2.9 0.9 %copy-done.3 = bf16[256,512]{1,0:T(8,128)(2,1)S(1)} copy-done((bf16[256,512]{1,0:T(8,128)(2,1)S(1)}, bf16[256,512]{1,0:T(8,128)(2,1)}, u32[]{:S(2)}) %copy-start.3) | copy-done | bytes 262168
  3.8 0.0 copy-start.4
  3.8 0.7 %copy-done.4 = f32[512]{0:T(512)S(1)} copy-done((f32[512]{0:T(512)S(1)}, f32[512]{0:T(512)}, u32[]{:S(2)}) %copy-start.4) | copy-done | bytes 2072
  4.5 49.2 %shard_map.55 = bf16[256,512]{1,0:T(8,128)(2,1)S(1)} custom-call(bf16[256,512]{1,0:T(8,128)(2,1)S(1)} %copy-done, bf16[256,512]{1,0:T(8,128)(2,1)S(1)} %copy-done.1, bf16[256,512]{1,0:T(8,128)(2,1)S(1)} %copy-done.2, bf16[256,512]{1,0:T(8,128)(2,1)S(1)} %copy-done.3, f32[1,512]{1,0:T(1,128)S(1)} %bitcast.1), custom_call_target="tpu_custom_call" | custom-call | tf_op jit(solution)/shard_map/pallas_call | solution.py:199
  53.7 0.7 %copy.7 = bf16[256,512]{1,0:T(8,128)(2,1)} copy(bf16[256,512]{1,0:T(8,128)(2,1)S(1)} %shard_map.55) | data formatting | bytes 524288
Async XLA Ops:
  0.0 0.9 %copy-start = (bf16[256,512]{1,0:T(8,128)(2,1)S(1)}, bf16[256,512]{1,0:T(8,128)(2,1)}, u32[]{:S(2)}) copy-start(bf16[256,512]{1,0:T(8,128)(2,1)} %in_gate.1) | copy-start | bytes 786436
  1.0 0.9 %copy-start.1 = (bf16[256,512]{1,0:T(8,128)(2,1)S(1)}, bf16[256,512]{1,0:T(8,128)(2,1)}, u32[]{:S(2)}) copy-start(bf16[256,512]{1,0:T(8,128)(2,1)} %values.1) | copy-start | bytes 786436
  1.9 0.9 %copy-start.2 = (bf16[256,512]{1,0:T(8,128)(2,1)S(1)}, bf16[256,512]{1,0:T(8,128)(2,1)}, u32[]{:S(2)}) copy-start(bf16[256,512]{1,0:T(8,128)(2,1)} %out_gate.1) | copy-start | bytes 786436
  2.9 0.9 %copy-start.3 = (bf16[256,512]{1,0:T(8,128)(2,1)S(1)}, bf16[256,512]{1,0:T(8,128)(2,1)}, u32[]{:S(2)}) copy-start(bf16[256,512]{1,0:T(8,128)(2,1)} %taps.1) | copy-start | bytes 786436
  3.8 0.7 %copy-start.4 = (f32[512]{0:T(512)S(1)}, f32[512]{0:T(512)}, u32[]{:S(2)}) copy-start(f32[512]{0:T(512)} %param.9) | copy-start | bytes 6148

commit v2 on v1

--- a/solution.py
+++ b/solution.py
@@ -11,16 +11,22 @@
 COARSE = 16
 FINE = 8
 CHUNK = 16
+TOGETHER = 4
 
 
 def kernel(
     devices,
+    in_gate_hbm,
+    values_hbm,
+    out_gate_hbm,
+    taps_hbm,
+    skip_gain_hbm,
+    mixed,
     in_gate,
     values,
     out_gate,
     taps,
     skip_gain,
-    mixed,
     sent,
     held,
     block,
@@ -31,7 +37,22 @@
     recv_sem,
     back_send_sem,
     back_recv_sem,
+    load_sem,
 ):
+    loads = [
+        pltpu.make_async_copy(source, target, load_sem.at[at])
+        for at, (source, target) in enumerate(
+            [
+                (taps_hbm, taps),
+                (in_gate_hbm, in_gate),
+                (values_hbm, values),
+                (out_gate_hbm, out_gate),
+                (skip_gain_hbm, skip_gain),
+            ]
+        )
+    ]
+    for load in loads:
+        load.start()
     own, channels = in_gate.shape
     share = channels // devices
     chunks = share // CHUNK
@@ -53,8 +74,11 @@
         == own - 1
     )
     flip = flip.astype(jnp.float32).astype(jnp.bfloat16)
+    loads[0].wait()
     taps_turned = taps[...].astype(jnp.float32).T.astype(jnp.bfloat16)
     taps_turned = jnp.dot(taps_turned, flip, preferred_element_type=jnp.float32)
+    loads[1].wait()
+    loads[2].wait()
     gated = in_gate[...].astype(jnp.float32) * values[...].astype(jnp.float32)
     gated = gated.T
     for u in range(per_owner):
@@ -107,7 +131,12 @@
     fine_mask = fine_lane + (FINE - 1) - fine_row < LANES
     wide_lane = lax.broadcasted_iota(jnp.int32, (COARSE, width), 1)
 
-    def convolve(chunk, at, carry):
+    def convolve(chunk, turn, carry):
+        for lane in range(TOGETHER):
+            convolve_one(chunk, turn * TOGETHER + lane)
+        return carry
+
+    def convolve_one(chunk, at):
         row = pl.ds(chunk * CHUNK + at, 1)
         pieces = []
         before = jnp.zeros((COARSE, LANES), jnp.float32)
@@ -149,12 +178,11 @@
             block[group, pl.ds(at, COARSE, stride=CHUNK), :] = total[
                 :, group * LANES : (group + 1) * LANES
             ]
-        return carry
 
     for chunk in range(chunks):
         for step in range(1, devices):
             forward(step, chunk).wait_recv()
-        lax.fori_loop(0, CHUNK, functools.partial(convolve, chunk), 0)
+        lax.fori_loop(0, CHUNK // TOGETHER, functools.partial(convolve, chunk), 0)
         for group in range(width // LANES):
             turned[chunk, group * LANES : (group + 1) * LANES, :] = block[group].T
         for step in range(1, devices):
@@ -167,6 +195,8 @@
             backward(step, chunk).wait_send()
             backward(step, chunk).wait_recv()
 
+    loads[3].wait()
+    loads[4].wait()
     parts = LANES // CHUNK
 
     def place(group, carry):
@@ -195,13 +225,17 @@
     chunks = share // CHUNK
     width = FINE * (own // LANES) * devices
     owned = FINE * (own // LANES)
-    vmem = pl.BlockSpec(memory_space=pltpu.VMEM)
     return pl.pallas_call(
         functools.partial(kernel, devices),
         out_shape=jax.ShapeDtypeStruct((own, channels), jnp.bfloat16),
-        in_specs=[vmem] * 5,
-        out_specs=vmem,
+        in_specs=[pl.BlockSpec(memory_space=pl.ANY)] * 5,
+        out_specs=pl.BlockSpec(memory_space=pltpu.VMEM),
         scratch_shapes=[
+            pltpu.VMEM((own, channels), jnp.bfloat16),
+            pltpu.VMEM((own, channels), jnp.bfloat16),
+            pltpu.VMEM((own, channels), jnp.bfloat16),
+            pltpu.VMEM((own, channels), jnp.bfloat16),
+            pltpu.VMEM((1, channels), jnp.float32),
             pltpu.VMEM((2, own // LANES, channels, LANES), jnp.float32),
             pltpu.VMEM((devices, 2, own // LANES, share, LANES), jnp.float32),
             pltpu.VMEM((width // LANES, COARSE * CHUNK, LANES), jnp.float32),
@@ -212,9 +246,10 @@
             pltpu.SemaphoreType.DMA((devices, chunks)),
             pltpu.SemaphoreType.DMA((devices, chunks)),
             pltpu.SemaphoreType.DMA((devices, chunks)),
+            pltpu.SemaphoreType.DMA((5,)),
         ],
         compiler_params=pltpu.CompilerParams(
-            collective_id=0, has_side_effects=True, vmem_limit_bytes=40 * 1024 * 1024
+            collective_id=0, has_side_effects=True, vmem_limit_bytes=60 * 1024 * 1024
         ),
     )(in_gate, values, out_gate, filter_taps, skip_gain.reshape(1, channels))
 

time: 54.7 us -> 46.8 us (0.86)
  Pallas kernels: 49.2 us -> 44.9 us
  local copies, waits for them, and re-layouts: 5.18 us -> 1.67 us
    pallas_call x1, Pallas kernels: 49.2 us -> 44.9 us  [local(): pl.pallas_call(functools.partial(kernel, devices), out_shape=jax.ShapeDty...]
    unnamed x11 -> x1, local copies, waits for them, and re-layouts: 5.18 us -> 1.67 us
where the time goes in v2:
time: 46.8 us; the launch traced here: 46.6 us
  Pallas kernels  44.9 us (96%)
  local copies, waits for them, and re-layouts  1.67 us (4%)
    pallas_call x1, Pallas kernels, local(): pl.pallas_call(functools.partial(kernel, devices), out_shape=jax.ShapeDty...  44.9 us
    unnamed x1, local copies, waits for them, and re-layouts  1.67 us

profile of v2, /device:TPU:0, one launch (start us, length us, event | category | flops | bytes accessed | tf_op | source)
XLA Modules:
  0.0 46.6 jit_solution(17125472108358120748)
XLA Ops:
  0.0 44.9 %shard_map.55 = bf16[256,512]{1,0:T(8,128)(2,1)} custom-call(bf16[256,512]{1,0:T(8,128)(2,1)} %in_gate_hbm.1, bf16[256,512]{1,0:T(8,128)(2,1)} %values_hbm.1, bf16[256,512]{1,0:T(8,128)(2,1)} %out_gate_hbm.1, bf16[256,512]{1,0:T(8,128)(2,1)} %taps_hbm.1, f32[1,512]{1,0:T(1,128)} %bitcast.1), custom_call_target="tpu_custom_call" | custom-call | tf_op jit(solution)/shard_map/pallas_call | solution.py:228
  44.9 1.7 %copy.7 = bf16[256,512]{1,0:T(8,128)(2,1)} copy(bf16[256,512]{1,0:T(8,128)(2,1)} %shard_map.55) | data formatting | bytes 524288

commit v3 on v2

v3 whole, which is shorter than its diff:
```python
import functools

import jax
import jax.numpy as jnp
from jax import lax
from jax.experimental import pallas as pl
from jax.experimental.pallas import tpu as pltpu
from jax.sharding import PartitionSpec as P

LANES = 128
COARSE = 16
FINE = 8
CHUNK = 16
TOGETHER = 4


def kernel(
    devices,
    groups,
    in_gate_hbm,
    values_hbm,
    taps_hbm,
    result,
    in_gate,
    values,
    taps,
    sent,
    signals,
    filters_held,
    block,
    turned,
    back,
    signal_send,
    signal_recv,
    filter_send,
    filter_recv,
    spread_send,
    spread_recv,
    back_send,
    back_recv,
    load_sem,
):
    loads = [
        pltpu.make_async_copy(source, target, load_sem.at[at])
        for at, (source, target) in enumerate(
            [
                (taps_hbm, taps),
                (in_gate_hbm, in_gate),
                (values_hbm, values),
            ]
        )
    ]
    for load in loads:
        load.start()
    own, channels = in_gate.shape
    share = channels // devices
    chunks = share // CHUNK
    per_owner = own // LANES
    count = per_owner * devices
    width = FINE * count
    me = lax.axis_index("seq")
    mine = lax.axis_index("grp")
    shared = chunks == groups and groups % 2 == 0
    pairs = max(groups // 2, 1)

    def group_at(turn, sign):
        if not shared:
            return turn
        pair = lax.rem(lax.div(mine, 2) + sign * (turn // 2) + pairs, pairs)
        return 2 * pair + lax.rem(lax.rem(mine, 2) + turn % 2, 2)

    barrier = pltpu.get_barrier_semaphore()
    for step in range(1, devices):
        peer = lax.rem(me + step, devices)
        pl.semaphore_signal(
            barrier, inc=1, device_id={"seq": peer}, device_id_type=pl.DeviceIdType.MESH
        )
    greeted = devices - 1
    if shared:
        for turn in range(1, groups):
            pl.semaphore_signal(
                barrier,
                inc=1,
                device_id={"grp": group_at(turn, 1)},
                device_id_type=pl.DeviceIdType.MESH,
            )
        greeted += groups - 1

    flip = (
        lax.broadcasted_iota(jnp.int32, (own, own), 0)
        + lax.broadcasted_iota(jnp.int32, (own, own), 1)
        == own - 1
    )
    flip = flip.astype(jnp.float32).astype(jnp.bfloat16)
    loads[0].wait()
    taps_turned = taps[...].astype(jnp.float32).T.astype(jnp.bfloat16)
    taps_turned = jnp.dot(taps_turned, flip, preferred_element_type=jnp.float32)
    loads[1].wait()
    loads[2].wait()
    gated = in_gate[...].astype(jnp.float32) * values[...].astype(jnp.float32)
    gated = gated.T
    for u in range(per_owner):
        sent[0, u] = gated[:, u * LANES : (u + 1) * LANES]
        sent[1, u] = taps_turned[:, u * LANES : (u + 1) * LANES]

    pl.semaphore_wait(barrier, greeted)

    def rows_of(device, chunk):
        return pl.ds(pl.multiple_of(device * share + chunk * CHUNK, CHUNK), CHUNK)

    def forward(which, step, turn):
        peer = lax.rem(me + step, devices)
        chunk = group_at(turn, 1)
        return pltpu.make_async_remote_copy(
            src_ref=sent.at[which, :, rows_of(peer, chunk), :],
            dst_ref=(signals, filters_held)[which].at[me, :, rows_of(0, chunk), :],
            send_sem=(signal_send, filter_send)[which].at[step, turn],
            recv_sem=(signal_recv, filter_recv)[which].at[step, turn],
            device_id={"seq": peer},
            device_id_type=pl.DeviceIdType.MESH,
        )

    def spread(turn):
        region = filters_held.at[:, :, rows_of(0, group_at(0, 1)), :]
        return pltpu.make_async_remote_copy(
            src_ref=region,
            dst_ref=region,
            send_sem=spread_send.at[turn],
            recv_sem=spread_recv.at[turn],
            device_id={"grp": group_at(turn, -1)},
            device_id_type=pl.DeviceIdType.MESH,
        )

    def owner_rows(device):
        start = FINE * per_owner * (devices - 1 - device)
        return pl.ds(pl.multiple_of(start, FINE * per_owner), FINE * per_owner)

    def backward(step, turn):
        peer = lax.rem(me + step, devices)
        return pltpu.make_async_remote_copy(
            src_ref=turned.at[turn, owner_rows(peer), :],
            dst_ref=back.at[me * chunks + group_at(turn, 1)],
            send_sem=back_send.at[step, turn],
            recv_sem=back_recv.at[step, turn],
            device_id={"seq": peer},
            device_id_type=pl.DeviceIdType.MESH,
        )

    filter_turns = 1 if shared else chunks
    for turn in range(chunks):
        for which in (1, 0):
            if which == 0 or turn < filter_turns:
                for step in range(1, devices):
                    forward(which, step, turn).start()
    for turn in range(chunks):
        chunk = group_at(turn, 1)
        signals[me, :, rows_of(0, chunk), :] = sent[0, :, rows_of(me, chunk), :]
        if turn < filter_turns:
            filters_held[me, :, rows_of(0, chunk), :] = sent[1, :, rows_of(me, chunk), :]

    coarse_row = lax.broadcasted_iota(jnp.int32, (COARSE, LANES), 0)
    coarse_lane = lax.broadcasted_iota(jnp.int32, (COARSE, LANES), 1)
    coarse_mask = coarse_lane >= FINE * coarse_row
    fine_row = lax.broadcasted_iota(jnp.int32, (FINE, LANES), 0)
    fine_lane = lax.broadcasted_iota(jnp.int32, (FINE, LANES), 1)
    fine_mask = fine_lane + (FINE - 1) - fine_row < LANES
    wide_lane = lax.broadcasted_iota(jnp.int32, (COARSE, width), 1)

    def convolve(chunk, few, carry):
        for lane in range(TOGETHER):
            convolve_one(chunk, few * TOGETHER + lane)
        return carry

    def convolve_one(chunk, at):
        row = pl.ds(chunk * CHUNK + at, 1)
        pieces = []
        before = jnp.zeros((COARSE, LANES), jnp.float32)
        for m in range(count):
            line = signals[m // per_owner, m % per_owner, row, :]
            rolled = pltpu.roll(
                jnp.broadcast_to(line, (COARSE, LANES)), 0, 1, stride=FINE, stride_axis=0
            )
            shifted = jnp.where(coarse_mask, rolled, before)
            before = rolled
            high = shifted.astype(jnp.bfloat16)
            low = (shifted - high.astype(jnp.float32)).astype(jnp.bfloat16)
            pieces.append(jnp.concatenate([high, low], axis=1))
        signal = jnp.concatenate(pieces, axis=0)
        pieces = []
        after = jnp.zeros((FINE, LANES), jnp.float32)
        for b in range(count - 1, -1, -1):
            line = filters_held[devices - 1 - b // per_owner, b % per_owner, row, :]
            rolled = pltpu.roll(
                jnp.broadcast_to(line, (FINE, LANES)),
                LANES - FINE + 1,
                1,
                stride=1,
                stride_axis=0,
            )
            pieces.append(jnp.where(fine_mask, rolled, after))
            after = rolled
        filters = jnp.concatenate(pieces[::-1], axis=0).astype(jnp.bfloat16)
        filters = jnp.concatenate([filters, filters], axis=1)
        product = lax.dot_general(
            signal, filters, (((1,), (1,)), ((), ())), preferred_element_type=jnp.float32
        )
        total = product[0:COARSE]
        for m in range(1, count):
            part = product[m * COARSE : (m + 1) * COARSE]
            part = jnp.where(wide_lane >= FINE * m, part, 0.0)
            total = total + pltpu.roll(part, width - FINE * m, 1)
        for group in range(width // LANES):
            block[group, pl.ds(at, COARSE, stride=CHUNK), :] = total[
                :, group * LANES : (group + 1) * LANES
            ]

    for turn in range(chunks):
        if turn < filter_turns:
            for step in range(1, devices):
                forward(1, step, turn).wait_recv()
        elif shared:
            spread(turn).wait_recv()
        if shared and turn == 0:
            for other in range(1, groups):
                spread(other).start()
        for step in range(1, devices):
            forward(0, step, turn).wait_recv()
        chunk = group_at(turn, 1)
        lax.fori_loop(0, CHUNK // TOGETHER, functools.partial(convolve, chunk), 0)
        for group in range(width // LANES):
            turned[turn, group * LANES : (group + 1) * LANES, :] = block[group].T
        for step in range(1, devices):
            backward(step, turn).start()
        back[me * chunks + chunk] = turned[turn, owner_rows(me), :]

    for turn in range(chunks):
        for step in range(1, devices):
            backward(step, turn).wait_recv()

    parts = LANES // CHUNK

    def place(group, carry):
        target = pl.ds(pl.multiple_of(group * LANES, LANES), LANES)
        for a in range(COARSE):
            lanes = pl.ds(a * CHUNK, CHUNK)
            merged = jnp.concatenate(
                [back[group * parts + part, :, lanes] for part in range(parts)], axis=1
            )
            for u in range(per_owner):
                start = LANES * (per_owner - 1 - u) + FINE * (COARSE - 1 - a)
                result[start : start + FINE, target] = merged[u * FINE : (u + 1) * FINE]
        return carry

    lax.fori_loop(0, channels // LANES, place, 0)
    for turn in range(chunks):
        for step in range(1, devices):
            forward(0, step, turn).wait_send()
            if turn < filter_turns:
                forward(1, step, turn).wait_send()
            backward(step, turn).wait_send()
    if shared:
        for turn in range(1, groups):
            spread(turn).wait_send()


def local(in_gate, values, out_gate, filter_taps, skip_gain):
    own, channels = in_gate.shape
    devices = lax.axis_size("seq")
    groups = lax.axis_size("grp")
    share = channels // devices
    chunks = share // CHUNK
    width = FINE * (own // LANES) * devices
    owned = FINE * (own // LANES)
    pieces = pltpu.SemaphoreType.DMA((devices, chunks))
    conv = pl.pallas_call(
        functools.partial(kernel, devices, groups),
        out_shape=jax.ShapeDtypeStruct((own, channels), jnp.float32),
        in_specs=[pl.BlockSpec(memory_space=pl.ANY)] * 3,
        out_specs=pl.BlockSpec(memory_space=pltpu.VMEM),
        scratch_shapes=[
            pltpu.VMEM((own, channels), jnp.bfloat16),
            pltpu.VMEM((own, channels), jnp.bfloat16),
            pltpu.VMEM((own, channels), jnp.bfloat16),
            pltpu.VMEM((2, own // LANES, channels, LANES), jnp.float32),
            pltpu.VMEM((devices, own // LANES, share, LANES), jnp.float32),
            pltpu.VMEM((devices, own // LANES, share, LANES), jnp.float32),
            pltpu.VMEM((width // LANES, COARSE * CHUNK, LANES), jnp.float32),
            pltpu.VMEM((chunks, width, COARSE * CHUNK), jnp.float32),
            pltpu.VMEM((devices * chunks, owned, COARSE * CHUNK), jnp.float32),
            pieces,
            pieces,
            pieces,
            pieces,
            pltpu.SemaphoreType.DMA((groups,)),
            pltpu.SemaphoreType.DMA((groups,)),
            pieces,
            pieces,
            pltpu.SemaphoreType.DMA((3,)),
        ],
        compiler_params=pltpu.CompilerParams(
            collective_id=0, has_side_effects=True, vmem_limit_bytes=60 * 1024 * 1024
        ),
    )(in_gate, values, filter_taps)
    gated = in_gate.astype(jnp.float32) * values.astype(jnp.float32)
    total = conv + skip_gain[None, :] * gated
    return (out_gate.astype(jnp.float32) * total).astype(jnp.bfloat16)


def solution(mesh):
    in_specs = (
        P(("grp", "seq"), None),
        P(("grp", "seq"), None),
        P(("grp", "seq"), None),
        P("seq", None),
        P(),
    )
    out_specs = P(("grp", "seq"), None)
    return jax.shard_map(local, mesh=mesh, in_specs=in_specs, out_specs=out_specs, check_vma=False)
```

time: 46.8 us -> 38.7 us (0.83)
  Pallas kernels: 44.9 us -> 36.6 us
  other arithmetic: 0 us -> 1.89 us
  local copies, waits for them, and re-layouts: 1.67 us -> 0.01 us
    pallas_call x1, Pallas kernels: 44.9 us -> 36.6 us  [local(): pl.pallas_call(functools.partial(kernel, devices, groups), out_shape=jax....]
    convert_element_type x0 -> x1, other arithmetic: none -> 1.89 us  [local(): return (out_gate.astype(jnp.float32) * total).astype(jnp.bfloat16)]
    unnamed x1 -> x8, local copies, waits for them, and re-layouts: 1.67 us -> 0.01 us
where the time goes in v3:
time: 38.7 us; the launch traced here: 38.5 us
  Pallas kernels  36.6 us (95%)
  other arithmetic  1.89 us (5%)
    pallas_call x1, Pallas kernels, local(): pl.pallas_call(functools.partial(kernel, devices, groups), out_shape=jax....  36.6 us
    convert_element_type x1, other arithmetic, local(): return (out_gate.astype(jnp.float32) * total).astype(jnp.bfloat16)  1.89 us

profile of v3, /device:TPU:0, one launch (start us, length us, event | category | flops | bytes accessed | tf_op | source)
XLA Modules:
  0.0 38.5 jit_solution(10509776347492009987)
XLA Ops:
  0.0 0.0 copy-start.1
  0.0 0.0 copy-start
  0.0 0.0 copy-start.3
  0.0 0.0 copy-start.2
  0.0 36.6 %shard_map.55 = f32[256,512]{1,0:T(8,128)} custom-call(bf16[256,512]{1,0:T(8,128)(2,1)} %in_gate_hbm.1, bf16[256,512]{1,0:T(8,128)(2,1)} %values_hbm.1, bf16[256,512]{1,0:T(8,128)(2,1)} %taps_hbm.1), custom_call_target="tpu_custom_call" | custom-call | tf_op jit(solution)/shard_map/pallas_call | solution.py:275
  36.6 0.0 copy-done.1
  36.6 0.0 copy-done
  36.6 0.0 copy-done.3
  36.6 0.0 copy-done.2
  36.6 1.9 %multiply_convert_fusion = bf16[256,512]{1,0:T(8,128)(2,1)} fusion(f32[256,512]{1,0:T(8,128)} %shard_map.55, bf16[256,512]{1,0:T(8,128)(2,1)S(1)} %copy-done.1, bf16[256,512]{1,0:T(8,128)(2,1)S(1)} %copy-done, bf16[256,512]{1,0:T(8,128)(2,1)S(1)} %copy-done.2, f32[512]{0:T(512)S(1)} %copy-done.3), kind=kLoop, calls=%fused_computation | loop fusion | flops 1048576 | bytes 1574912 | tf_op jit(solution)/shard_map/convert_element_type | solution.py:306
Async XLA Ops:
  0.0 36.6 %copy-start.1 = (bf16[256,512]{1,0:T(8,128)(2,1)S(1)}, bf16[256,512]{1,0:T(8,128)(2,1)}, u32[]{:S(2)}) copy-start(bf16[256,512]{1,0:T(8,128)(2,1)} %values_hbm.1) | copy-start | bytes 786436
  0.0 36.6 %copy-start = (bf16[256,512]{1,0:T(8,128)(2,1)S(1)}, bf16[256,512]{1,0:T(8,128)(2,1)}, u32[]{:S(2)}) copy-start(bf16[256,512]{1,0:T(8,128)(2,1)} %in_gate_hbm.1) | copy-start | bytes 786436
  0.0 36.6 %copy-start.3 = (f32[512]{0:T(512)S(1)}, f32[512]{0:T(512)}, u32[]{:S(2)}) copy-start(f32[512]{0:T(512)} %param.9) | copy-start | bytes 6148
  0.0 36.6 %copy-start.2 = (bf16[256,512]{1,0:T(8,128)(2,1)S(1)}, bf16[256,512]{1,0:T(8,128)(2,1)}, u32[]{:S(2)}) copy-start(bf16[256,512]{1,0:T(8,128)(2,1)} %param.7) | copy-start | bytes 786436

commit v4 on v3

--- a/solution.py
+++ b/solution.py
@@ -11,7 +11,7 @@
 COARSE = 16
 FINE = 8
 CHUNK = 16
-TOGETHER = 4
+TOGETHER = 8
 
 
 def kernel(
@@ -44,9 +44,9 @@
         pltpu.make_async_copy(source, target, load_sem.at[at])
         for at, (source, target) in enumerate(
             [
-                (taps_hbm, taps),
                 (in_gate_hbm, in_gate),
                 (values_hbm, values),
+                (taps_hbm, taps),
             ]
         )
     ]
@@ -86,22 +86,12 @@
             )
         greeted += groups - 1
 
-    flip = (
-        lax.broadcasted_iota(jnp.int32, (own, own), 0)
-        + lax.broadcasted_iota(jnp.int32, (own, own), 1)
-        == own - 1
-    )
-    flip = flip.astype(jnp.float32).astype(jnp.bfloat16)
     loads[0].wait()
-    taps_turned = taps[...].astype(jnp.float32).T.astype(jnp.bfloat16)
-    taps_turned = jnp.dot(taps_turned, flip, preferred_element_type=jnp.float32)
     loads[1].wait()
-    loads[2].wait()
     gated = in_gate[...].astype(jnp.float32) * values[...].astype(jnp.float32)
     gated = gated.T
     for u in range(per_owner):
         sent[0, u] = gated[:, u * LANES : (u + 1) * LANES]
-        sent[1, u] = taps_turned[:, u * LANES : (u + 1) * LANES]
 
     pl.semaphore_wait(barrier, greeted)
 
@@ -146,10 +136,25 @@
             device_id_type=pl.DeviceIdType.MESH,
         )
 
+    for step in range(1, devices):
+        forward(0, step, 0).start()
+
+    flip = (
+        lax.broadcasted_iota(jnp.int32, (own, own), 0)
+        + lax.broadcasted_iota(jnp.int32, (own, own), 1)
+        == own - 1
+    )
+    flip = flip.astype(jnp.float32).astype(jnp.bfloat16)
+    loads[2].wait()
+    taps_turned = taps[...].astype(jnp.float32).T.astype(jnp.bfloat16)
+    taps_turned = jnp.dot(taps_turned, flip, preferred_element_type=jnp.float32)
+    for u in range(per_owner):
+        sent[1, u] = taps_turned[:, u * LANES : (u + 1) * LANES]
+
     filter_turns = 1 if shared else chunks
     for turn in range(chunks):
         for which in (1, 0):
-            if which == 0 or turn < filter_turns:
+            if (which == 0 and turn > 0) or (which == 1 and turn < filter_turns):
                 for step in range(1, devices):
                     forward(which, step, turn).start()
     for turn in range(chunks):

time: 38.7 us -> 39.9 us (1.031)
  Pallas kernels: 36.6 us -> 37.8 us
    pallas_call x1, Pallas kernels: 36.6 us -> 37.8 us  [local(): pl.pallas_call(functools.partial(kernel, devices, groups), out_shape=jax....]
where the time goes in v4:
time: 39.9 us; the launch traced here: 39.7 us
  Pallas kernels  37.8 us (95%)
  other arithmetic  1.89 us (5%)
    pallas_call x1, Pallas kernels, local(): pl.pallas_call(functools.partial(kernel, devices, groups), out_shape=jax....  37.8 us
    convert_element_type x1, other arithmetic, local(): return (out_gate.astype(jnp.float32) * total).astype(jnp.bfloat16)  1.89 us

profile of v4, /device:TPU:0, one launch (start us, length us, event | category | flops | bytes accessed | tf_op | source)
XLA Modules:
  0.0 39.7 jit_solution(8927602995157632462)
XLA Ops:
  0.0 0.0 copy-start.1
  0.0 0.0 copy-start
  0.0 0.0 copy-start.3
  0.0 0.0 copy-start.2
  0.0 37.8 %shard_map.55 = f32[256,512]{1,0:T(8,128)} custom-call(bf16[256,512]{1,0:T(8,128)(2,1)} %in_gate_hbm.1, bf16[256,512]{1,0:T(8,128)(2,1)} %values_hbm.1, bf16[256,512]{1,0:T(8,128)(2,1)} %taps_hbm.1), custom_call_target="tpu_custom_call" | custom-call | tf_op jit(solution)/shard_map/pallas_call | solution.py:280
  37.8 0.0 copy-done.1
  37.8 0.0 copy-done
  37.8 0.0 copy-done.3
  37.8 0.0 copy-done.2
  37.9 1.9 %multiply_convert_fusion = bf16[256,512]{1,0:T(8,128)(2,1)} fusion(f32[256,512]{1,0:T(8,128)} %shard_map.55, bf16[256,512]{1,0:T(8,128)(2,1)S(1)} %copy-done.1, bf16[256,512]{1,0:T(8,128)(2,1)S(1)} %copy-done, bf16[256,512]{1,0:T(8,128)(2,1)S(1)} %copy-done.2, f32[512]{0:T(512)S(1)} %copy-done.3), kind=kLoop, calls=%fused_computation | loop fusion | flops 1048576 | bytes 1574912 | tf_op jit(solution)/shard_map/convert_element_type | solution.py:311
Async XLA Ops:
  0.0 37.8 %copy-start.1 = (bf16[256,512]{1,0:T(8,128)(2,1)S(1)}, bf16[256,512]{1,0:T(8,128)(2,1)}, u32[]{:S(2)}) copy-start(bf16[256,512]{1,0:T(8,128)(2,1)} %values_hbm.1) | copy-start | bytes 786436
  0.0 37.8 %copy-start = (bf16[256,512]{1,0:T(8,128)(2,1)S(1)}, bf16[256,512]{1,0:T(8,128)(2,1)}, u32[]{:S(2)}) copy-start(bf16[256,512]{1,0:T(8,128)(2,1)} %in_gate_hbm.1) | copy-start | bytes 786436
  0.0 37.8 %copy-start.3 = (f32[512]{0:T(512)S(1)}, f32[512]{0:T(512)}, u32[]{:S(2)}) copy-start(f32[512]{0:T(512)} %param.9) | copy-start | bytes 6148
  0.0 37.8 %copy-start.2 = (bf16[256,512]{1,0:T(8,128)(2,1)S(1)}, bf16[256,512]{1,0:T(8,128)(2,1)}, u32[]{:S(2)}) copy-start(bf16[256,512]{1,0:T(8,128)(2,1)} %param.7) | copy-start | bytes 786436

commit v5 on v3

--- a/solution.py
+++ b/solution.py
@@ -39,6 +39,8 @@
     back_send,
     back_recv,
     load_sem,
+    placed,
+    placed_sem,
 ):
     loads = [
         pltpu.make_async_copy(source, target, load_sem.at[at])
@@ -60,6 +62,17 @@
     width = FINE * count
     me = lax.axis_index("seq")
     mine = lax.axis_index("grp")
+    half = devices // 2
+    order = [step for at in range(half) for step in (half + at, 1 + at)][: devices - 1]
+
+    def partner(step):
+        peer, bit = me * 0, 1
+        while bit < devices:
+            own_bit = lax.rem(lax.div(me, bit), 2)
+            peer = peer + bit * (1 - own_bit if step & bit else own_bit)
+            bit *= 2
+        return peer
+
     shared = chunks == groups and groups % 2 == 0
     pairs = max(groups // 2, 1)
 
@@ -70,8 +83,8 @@
         return 2 * pair + lax.rem(lax.rem(mine, 2) + turn % 2, 2)
 
     barrier = pltpu.get_barrier_semaphore()
-    for step in range(1, devices):
-        peer = lax.rem(me + step, devices)
+    for step in order:
+        peer = partner(step)
         pl.semaphore_signal(
             barrier, inc=1, device_id={"seq": peer}, device_id_type=pl.DeviceIdType.MESH
         )
@@ -109,7 +122,7 @@
         return pl.ds(pl.multiple_of(device * share + chunk * CHUNK, CHUNK), CHUNK)
 
     def forward(which, step, turn):
-        peer = lax.rem(me + step, devices)
+        peer = partner(step)
         chunk = group_at(turn, 1)
         return pltpu.make_async_remote_copy(
             src_ref=sent.at[which, :, rows_of(peer, chunk), :],
@@ -136,7 +149,7 @@
         return pl.ds(pl.multiple_of(start, FINE * per_owner), FINE * per_owner)
 
     def backward(step, turn):
-        peer = lax.rem(me + step, devices)
+        peer = partner(step)
         return pltpu.make_async_remote_copy(
             src_ref=turned.at[turn, owner_rows(peer), :],
             dst_ref=back.at[me * chunks + group_at(turn, 1)],
@@ -150,7 +163,7 @@
     for turn in range(chunks):
         for which in (1, 0):
             if which == 0 or turn < filter_turns:
-                for step in range(1, devices):
+                for step in order:
                     forward(which, step, turn).start()
     for turn in range(chunks):
         chunk = group_at(turn, 1)
@@ -216,31 +229,36 @@
 
     for turn in range(chunks):
         if turn < filter_turns:
-            for step in range(1, devices):
+            for step in order:
                 forward(1, step, turn).wait_recv()
         elif shared:
             spread(turn).wait_recv()
         if shared and turn == 0:
             for other in range(1, groups):
                 spread(other).start()
-        for step in range(1, devices):
+        for step in order:
             forward(0, step, turn).wait_recv()
         chunk = group_at(turn, 1)
         lax.fori_loop(0, CHUNK // TOGETHER, functools.partial(convolve, chunk), 0)
         for group in range(width // LANES):
             turned[turn, group * LANES : (group + 1) * LANES, :] = block[group].T
-        for step in range(1, devices):
+        for step in order:
             backward(step, turn).start()
         back[me * chunks + chunk] = turned[turn, owner_rows(me), :]
 
     for turn in range(chunks):
-        for step in range(1, devices):
+        for step in order:
             backward(step, turn).wait_recv()
 
     parts = LANES // CHUNK
 
+    def store(group):
+        target = pl.ds(pl.multiple_of(group * LANES, LANES), LANES)
+        return pltpu.make_async_copy(
+            placed.at[group], result.at[:, target], placed_sem.at[group]
+        )
+
     def place(group, carry):
-        target = pl.ds(pl.multiple_of(group * LANES, LANES), LANES)
         for a in range(COARSE):
             lanes = pl.ds(a * CHUNK, CHUNK)
             merged = jnp.concatenate(
@@ -248,12 +266,13 @@
             )
             for u in range(per_owner):
                 start = LANES * (per_owner - 1 - u) + FINE * (COARSE - 1 - a)
-                result[start : start + FINE, target] = merged[u * FINE : (u + 1) * FINE]
+                placed[group, start : start + FINE, :] = merged[u * FINE : (u + 1) * FINE]
+        store(group).start()
         return carry
 
     lax.fori_loop(0, channels // LANES, place, 0)
     for turn in range(chunks):
-        for step in range(1, devices):
+        for step in order:
             forward(0, step, turn).wait_send()
             if turn < filter_turns:
                 forward(1, step, turn).wait_send()
@@ -261,6 +280,8 @@
     if shared:
         for turn in range(1, groups):
             spread(turn).wait_send()
+    for group in range(channels // LANES):
+        store(group).wait()
 
 
 def local(in_gate, values, out_gate, filter_taps, skip_gain):
@@ -276,7 +297,7 @@
         functools.partial(kernel, devices, groups),
         out_shape=jax.ShapeDtypeStruct((own, channels), jnp.float32),
         in_specs=[pl.BlockSpec(memory_space=pl.ANY)] * 3,
-        out_specs=pl.BlockSpec(memory_space=pltpu.VMEM),
+        out_specs=pl.BlockSpec(memory_space=pl.ANY),
         scratch_shapes=[
             pltpu.VMEM((own, channels), jnp.bfloat16),
             pltpu.VMEM((own, channels), jnp.bfloat16),
@@ -296,6 +317,8 @@
             pieces,
             pieces,
             pltpu.SemaphoreType.DMA((3,)),
+            pltpu.VMEM((channels // LANES, own, LANES), jnp.float32),
+            pltpu.SemaphoreType.DMA((channels // LANES,)),
         ],
         compiler_params=pltpu.CompilerParams(
             collective_id=0, has_side_effects=True, vmem_limit_bytes=60 * 1024 * 1024

time: 38.7 us -> 38.6 us (level)
  no operation moved by 1% of the time
where the time goes in v5:
time: 38.6 us; the launch traced here: 38.4 us
  Pallas kernels  36.5 us (95%)
  other arithmetic  1.89 us (5%)
    pallas_call x1, Pallas kernels, local(): pl.pallas_call(functools.partial(kernel, devices, groups), out_shape=jax....  36.5 us
    convert_element_type x1, other arithmetic, local(): return (out_gate.astype(jnp.float32) * total).astype(jnp.bfloat16)  1.89 us

profile of v5, /device:TPU:0, one launch (start us, length us, event | category | flops | bytes accessed | tf_op | source)
XLA Modules:
  0.0 38.4 jit_solution(11724621677690775223)
XLA Ops:
  0.0 0.0 copy-start.1
  0.0 0.0 copy-start
  0.0 0.0 copy-start.3
  0.0 0.0 copy-start.2
  0.0 36.5 %shard_map.55 = f32[256,512]{1,0:T(8,128)} custom-call(bf16[256,512]{1,0:T(8,128)(2,1)} %in_gate_hbm.1, bf16[256,512]{1,0:T(8,128)(2,1)} %values_hbm.1, bf16[256,512]{1,0:T(8,128)(2,1)} %taps_hbm.1), custom_call_target="tpu_custom_call" | custom-call | tf_op jit(solution)/shard_map/pallas_call | solution.py:296
  36.5 0.0 copy-done.1
  36.5 0.0 copy-done
  36.5 0.0 copy-done.3
  36.5 0.0 copy-done.2
  36.5 1.9 %multiply_convert_fusion = bf16[256,512]{1,0:T(8,128)(2,1)} fusion(f32[256,512]{1,0:T(8,128)} %shard_map.55, bf16[256,512]{1,0:T(8,128)(2,1)S(1)} %copy-done.1, bf16[256,512]{1,0:T(8,128)(2,1)S(1)} %copy-done, bf16[256,512]{1,0:T(8,128)(2,1)S(1)} %copy-done.2, f32[512]{0:T(512)S(1)} %copy-done.3), kind=kLoop, calls=%fused_computation | loop fusion | flops 1048576 | bytes 1574912 | tf_op jit(solution)/shard_map/convert_element_type | solution.py:329
Async XLA Ops:
  0.0 36.5 %copy-start.1 = (bf16[256,512]{1,0:T(8,128)(2,1)S(1)}, bf16[256,512]{1,0:T(8,128)(2,1)}, u32[]{:S(2)}) copy-start(bf16[256,512]{1,0:T(8,128)(2,1)} %values_hbm.1) | copy-start | bytes 786436
  0.0 36.5 %copy-start = (bf16[256,512]{1,0:T(8,128)(2,1)S(1)}, bf16[256,512]{1,0:T(8,128)(2,1)}, u32[]{:S(2)}) copy-start(bf16[256,512]{1,0:T(8,128)(2,1)} %in_gate_hbm.1) | copy-start | bytes 786436
  0.0 36.5 %copy-start.3 = (f32[512]{0:T(512)S(1)}, f32[512]{0:T(512)}, u32[]{:S(2)}) copy-start(f32[512]{0:T(512)} %param.9) | copy-start | bytes 6148
  0.0 36.5 %copy-start.2 = (bf16[256,512]{1,0:T(8,128)(2,1)S(1)}, bf16[256,512]{1,0:T(8,128)(2,1)}, u32[]{:S(2)}) copy-start(bf16[256,512]{1,0:T(8,128)(2,1)} %param.7) | copy-start | bytes 786436

commit v6 on v5

--- a/solution.py
+++ b/solution.py
@@ -46,9 +46,9 @@
         pltpu.make_async_copy(source, target, load_sem.at[at])
         for at, (source, target) in enumerate(
             [
-                (taps_hbm, taps),
                 (in_gate_hbm, in_gate),
                 (values_hbm, values),
+                (taps_hbm, taps),
             ]
         )
     ]
@@ -99,34 +99,49 @@
             )
         greeted += groups - 1
 
-    flip = (
-        lax.broadcasted_iota(jnp.int32, (own, own), 0)
-        + lax.broadcasted_iota(jnp.int32, (own, own), 1)
-        == own - 1
-    )
-    flip = flip.astype(jnp.float32).astype(jnp.bfloat16)
+    reach = devices * CHUNK
+
+    def columns_of(chunk):
+        return pl.ds(pl.multiple_of(chunk * reach, LANES), reach)
+
+    def turn_signal(turn):
+        columns = columns_of(group_at(turn, 1))
+        gated = in_gate[:, columns].astype(jnp.float32) * values[:, columns].astype(jnp.float32)
+        gated = gated.T
+        for u in range(per_owner):
+            sent[0, u, columns, :] = gated[:, u * LANES : (u + 1) * LANES]
+
+    def turn_filter(turn):
+        columns = columns_of(group_at(turn, 1))
+        flip = (
+            lax.broadcasted_iota(jnp.int32, (own, own), 0)
+            + lax.broadcasted_iota(jnp.int32, (own, own), 1)
+            == own - 1
+        )
+        flip = flip.astype(jnp.float32).astype(jnp.bfloat16)
+        turned_taps = taps[:, columns].astype(jnp.float32).T.astype(jnp.bfloat16)
+        turned_taps = jnp.dot(turned_taps, flip, preferred_element_type=jnp.float32)
+        for u in range(per_owner):
+            sent[1, u, columns, :] = turned_taps[:, u * LANES : (u + 1) * LANES]
+
     loads[0].wait()
-    taps_turned = taps[...].astype(jnp.float32).T.astype(jnp.bfloat16)
-    taps_turned = jnp.dot(taps_turned, flip, preferred_element_type=jnp.float32)
     loads[1].wait()
-    loads[2].wait()
-    gated = in_gate[...].astype(jnp.float32) * values[...].astype(jnp.float32)
-    gated = gated.T
-    for u in range(per_owner):
-        sent[0, u] = gated[:, u * LANES : (u + 1) * LANES]
-        sent[1, u] = taps_turned[:, u * LANES : (u + 1) * LANES]
+    turn_signal(0)
 
     pl.semaphore_wait(barrier, greeted)
 
     def rows_of(device, chunk):
-        return pl.ds(pl.multiple_of(device * share + chunk * CHUNK, CHUNK), CHUNK)
+        return pl.ds(pl.multiple_of((chunk * devices + device) * CHUNK, CHUNK), CHUNK)
+
+    def rows_in(chunk):
+        return pl.ds(pl.multiple_of(chunk * CHUNK, CHUNK), CHUNK)
 
     def forward(which, step, turn):
         peer = partner(step)
         chunk = group_at(turn, 1)
         return pltpu.make_async_remote_copy(
             src_ref=sent.at[which, :, rows_of(peer, chunk), :],
-            dst_ref=(signals, filters_held)[which].at[me, :, rows_of(0, chunk), :],
+            dst_ref=(signals, filters_held)[which].at[me, :, rows_in(chunk), :],
             send_sem=(signal_send, filter_send)[which].at[step, turn],
             recv_sem=(signal_recv, filter_recv)[which].at[step, turn],
             device_id={"seq": peer},
@@ -134,7 +149,7 @@
         )
 
     def spread(turn):
-        region = filters_held.at[:, :, rows_of(0, group_at(0, 1)), :]
+        region = filters_held.at[:, :, rows_in(group_at(0, 1)), :]
         return pltpu.make_async_remote_copy(
             src_ref=region,
             dst_ref=region,
@@ -152,7 +167,7 @@
         peer = partner(step)
         return pltpu.make_async_remote_copy(
             src_ref=turned.at[turn, owner_rows(peer), :],
-            dst_ref=back.at[me * chunks + group_at(turn, 1)],
+            dst_ref=back.at[group_at(turn, 1) * devices + me],
             send_sem=back_send.at[step, turn],
             recv_sem=back_recv.at[step, turn],
             device_id={"seq": peer},
@@ -161,15 +176,21 @@
 
     filter_turns = 1 if shared else chunks
     for turn in range(chunks):
-        for which in (1, 0):
-            if which == 0 or turn < filter_turns:
-                for step in order:
-                    forward(which, step, turn).start()
+        if turn > 0:
+            turn_signal(turn)
+        for step in order:
+            forward(0, step, turn).start()
+        if turn < filter_turns:
+            if turn == 0:
+                loads[2].wait()
+            turn_filter(turn)
+            for step in order:
+                forward(1, step, turn).start()
     for turn in range(chunks):
         chunk = group_at(turn, 1)
-        signals[me, :, rows_of(0, chunk), :] = sent[0, :, rows_of(me, chunk), :]
+        signals[me, :, rows_in(chunk), :] = sent[0, :, rows_of(me, chunk), :]
         if turn < filter_turns:
-            filters_held[me, :, rows_of(0, chunk), :] = sent[1, :, rows_of(me, chunk), :]
+            filters_held[me, :, rows_in(chunk), :] = sent[1, :, rows_of(me, chunk), :]
 
     coarse_row = lax.broadcasted_iota(jnp.int32, (COARSE, LANES), 0)
     coarse_lane = lax.broadcasted_iota(jnp.int32, (COARSE, LANES), 1)
@@ -244,11 +265,7 @@
             turned[turn, group * LANES : (group + 1) * LANES, :] = block[group].T
         for step in order:
             backward(step, turn).start()
-        back[me * chunks + chunk] = turned[turn, owner_rows(me), :]
-
-    for turn in range(chunks):
-        for step in order:
-            backward(step, turn).wait_recv()
+        back[chunk * devices + me] = turned[turn, owner_rows(me), :]
 
     parts = LANES // CHUNK
 
@@ -270,7 +287,11 @@
         store(group).start()
         return carry
 
-    lax.fori_loop(0, channels // LANES, place, 0)
+    for turn in range(chunks):
+        for step in order:
+            backward(step, turn).wait_recv()
+        first = group_at(turn, 1) * (reach // LANES)
+        lax.fori_loop(first, first + reach // LANES, place, 0)
     for turn in range(chunks):
         for step in order:
             forward(0, step, turn).wait_send()

time: 38.6 us -> 37.7 us (0.977)
  Pallas kernels: 36.5 us -> 35.6 us
    pallas_call x1, Pallas kernels: 36.5 us -> 35.6 us  [local(): pl.pallas_call(functools.partial(kernel, devices, groups), out_shape=jax....]
where the time goes in v6:
time: 37.7 us; the launch traced here: 37.5 us
  Pallas kernels  35.6 us (94%)
  other arithmetic  1.89 us (5%)
    pallas_call x1, Pallas kernels, local(): pl.pallas_call(functools.partial(kernel, devices, groups), out_shape=jax....  35.6 us
    convert_element_type x1, other arithmetic, local(): return (out_gate.astype(jnp.float32) * total).astype(jnp.bfloat16)  1.89 us

profile of v6, /device:TPU:0, one launch (start us, length us, event | category | flops | bytes accessed | tf_op | source)
XLA Modules:
  0.0 37.5 jit_solution(8886147033991518138)
XLA Ops:
  0.0 0.0 copy-start.1
  0.0 0.0 copy-start
  0.0 0.0 copy-start.3
  0.0 0.0 copy-start.2
  0.0 35.6 %shard_map.55 = f32[256,512]{1,0:T(8,128)} custom-call(bf16[256,512]{1,0:T(8,128)(2,1)} %in_gate_hbm.1, bf16[256,512]{1,0:T(8,128)(2,1)} %values_hbm.1, bf16[256,512]{1,0:T(8,128)(2,1)} %taps_hbm.1), custom_call_target="tpu_custom_call" | custom-call | tf_op jit(solution)/shard_map/pallas_call | solution.py:317
  35.6 0.0 copy-done.1
  35.6 0.0 copy-done
  35.6 0.0 copy-done.3
  35.6 0.0 copy-done.2
  35.6 1.9 %multiply_convert_fusion = bf16[256,512]{1,0:T(8,128)(2,1)} fusion(f32[256,512]{1,0:T(8,128)} %shard_map.55, bf16[256,512]{1,0:T(8,128)(2,1)S(1)} %copy-done.1, bf16[256,512]{1,0:T(8,128)(2,1)S(1)} %copy-done, bf16[256,512]{1,0:T(8,128)(2,1)S(1)} %copy-done.2, f32[512]{0:T(512)S(1)} %copy-done.3), kind=kLoop, calls=%fused_computation | loop fusion | flops 1048576 | bytes 1574912 | tf_op jit(solution)/shard_map/convert_element_type | solution.py:350
Async XLA Ops:
  0.0 35.6 %copy-start.1 = (bf16[256,512]{1,0:T(8,128)(2,1)S(1)}, bf16[256,512]{1,0:T(8,128)(2,1)}, u32[]{:S(2)}) copy-start(bf16[256,512]{1,0:T(8,128)(2,1)} %values_hbm.1) | copy-start | bytes 786436
  0.0 35.6 %copy-start = (bf16[256,512]{1,0:T(8,128)(2,1)S(1)}, bf16[256,512]{1,0:T(8,128)(2,1)}, u32[]{:S(2)}) copy-start(bf16[256,512]{1,0:T(8,128)(2,1)} %in_gate_hbm.1) | copy-start | bytes 786436
  0.0 35.6 %copy-start.3 = (f32[512]{0:T(512)S(1)}, f32[512]{0:T(512)}, u32[]{:S(2)}) copy-start(f32[512]{0:T(512)} %param.9) | copy-start | bytes 6148
  0.0 35.6 %copy-start.2 = (bf16[256,512]{1,0:T(8,128)(2,1)S(1)}, bf16[256,512]{1,0:T(8,128)(2,1)}, u32[]{:S(2)}) copy-start(bf16[256,512]{1,0:T(8,128)(2,1)} %param.7) | copy-start | bytes 786436

commit v7 on v6

--- a/solution.py
+++ b/solution.py
@@ -8,8 +8,8 @@
 from jax.sharding import PartitionSpec as P
 
 LANES = 128
-COARSE = 16
-FINE = 8
+COARSE = 8
+FINE = 16
 CHUNK = 16
 TOGETHER = 4
 
@@ -216,10 +216,11 @@
             )
             shifted = jnp.where(coarse_mask, rolled, before)
             before = rolled
-            high = shifted.astype(jnp.bfloat16)
-            low = (shifted - high.astype(jnp.float32)).astype(jnp.bfloat16)
-            pieces.append(jnp.concatenate([high, low], axis=1))
+            pieces.append(shifted)
         signal = jnp.concatenate(pieces, axis=0)
+        high = signal.astype(jnp.bfloat16)
+        low = (signal - high.astype(jnp.float32)).astype(jnp.bfloat16)
+        signal = jnp.concatenate([high, low], axis=1)
         pieces = []
         after = jnp.zeros((FINE, LANES), jnp.float32)
         for b in range(count - 1, -1, -1):

time: 37.7 us -> 37.7 us (level)
  no operation moved by 1% of the time
where the time goes in v7:
time: 37.7 us; the launch traced here: 37.6 us
  Pallas kernels  35.6 us (94%)
  other arithmetic  1.89 us (5%)
    pallas_call x1, Pallas kernels, local(): pl.pallas_call(functools.partial(kernel, devices, groups), out_shape=jax....  35.6 us
    convert_element_type x1, other arithmetic, local(): return (out_gate.astype(jnp.float32) * total).astype(jnp.bfloat16)  1.89 us

profile of v7, /device:TPU:0, one launch (start us, length us, event | category | flops | bytes accessed | tf_op | source)
XLA Modules:
  0.0 37.6 jit_solution(14491208806268958806)
XLA Ops:
  0.0 0.0 copy-start.1
  0.0 0.0 copy-start
  0.0 0.0 copy-start.3
  0.0 0.0 copy-start.2
  0.0 35.6 %shard_map.55 = f32[256,512]{1,0:T(8,128)} custom-call(bf16[256,512]{1,0:T(8,128)(2,1)} %in_gate_hbm.1, bf16[256,512]{1,0:T(8,128)(2,1)} %values_hbm.1, bf16[256,512]{1,0:T(8,128)(2,1)} %taps_hbm.1), custom_call_target="tpu_custom_call" | custom-call | tf_op jit(solution)/shard_map/pallas_call | solution.py:318
  35.6 0.0 copy-done.1
  35.6 0.0 copy-done
  35.6 0.0 copy-done.3
  35.7 0.0 copy-done.2
  35.7 1.9 %multiply_convert_fusion = bf16[256,512]{1,0:T(8,128)(2,1)} fusion(f32[256,512]{1,0:T(8,128)} %shard_map.55, bf16[256,512]{1,0:T(8,128)(2,1)S(1)} %copy-done.1, bf16[256,512]{1,0:T(8,128)(2,1)S(1)} %copy-done, bf16[256,512]{1,0:T(8,128)(2,1)S(1)} %copy-done.2, f32[512]{0:T(512)S(1)} %copy-done.3), kind=kLoop, calls=%fused_computation | loop fusion | flops 1048576 | bytes 1574912 | tf_op jit(solution)/shard_map/convert_element_type | solution.py:351
Async XLA Ops:
  0.0 35.6 %copy-start.1 = (bf16[256,512]{1,0:T(8,128)(2,1)S(1)}, bf16[256,512]{1,0:T(8,128)(2,1)}, u32[]{:S(2)}) copy-start(bf16[256,512]{1,0:T(8,128)(2,1)} %values_hbm.1) | copy-start | bytes 786436
  0.0 35.6 %copy-start = (bf16[256,512]{1,0:T(8,128)(2,1)S(1)}, bf16[256,512]{1,0:T(8,128)(2,1)}, u32[]{:S(2)}) copy-start(bf16[256,512]{1,0:T(8,128)(2,1)} %in_gate_hbm.1) | copy-start | bytes 786436
  0.0 35.6 %copy-start.3 = (f32[512]{0:T(512)S(1)}, f32[512]{0:T(512)}, u32[]{:S(2)}) copy-start(f32[512]{0:T(512)} %param.9) | copy-start | bytes 6148
  0.0 35.7 %copy-start.2 = (bf16[256,512]{1,0:T(8,128)(2,1)S(1)}, bf16[256,512]{1,0:T(8,128)(2,1)}, u32[]{:S(2)}) copy-start(bf16[256,512]{1,0:T(8,128)(2,1)} %param.7) | copy-start | bytes 786436

commit v8 on v7

--- a/solution.py
+++ b/solution.py
@@ -263,7 +263,7 @@
         chunk = group_at(turn, 1)
         lax.fori_loop(0, CHUNK // TOGETHER, functools.partial(convolve, chunk), 0)
         for group in range(width // LANES):
-            turned[turn, group * LANES : (group + 1) * LANES, :] = block[group].T
+            turned[turn, group * LANES : (group + 1) * LANES, :] = block[group, : COARSE * CHUNK].T
         for step in order:
             backward(step, turn).start()
         back[chunk * devices + me] = turned[turn, owner_rows(me), :]
@@ -327,7 +327,7 @@
             pltpu.VMEM((2, own // LANES, channels, LANES), jnp.float32),
             pltpu.VMEM((devices, own // LANES, share, LANES), jnp.float32),
             pltpu.VMEM((devices, own // LANES, share, LANES), jnp.float32),
-            pltpu.VMEM((width // LANES, COARSE * CHUNK, LANES), jnp.float32),
+            pltpu.VMEM((width // LANES, (COARSE + 1) * CHUNK, LANES), jnp.float32),
             pltpu.VMEM((chunks, width, COARSE * CHUNK), jnp.float32),
             pltpu.VMEM((devices * chunks, owned, COARSE * CHUNK), jnp.float32),
             pieces,

time: 37.7 us -> 37.7 us (level)
  no operation moved by 1% of the time
where the time goes in v8:
time: 37.7 us; the launch traced here: 37.6 us
  Pallas kernels  35.6 us (94%)
  other arithmetic  1.89 us (5%)
    pallas_call x1, Pallas kernels, local(): pl.pallas_call(functools.partial(kernel, devices, groups), out_shape=jax....  35.6 us
    convert_element_type x1, other arithmetic, local(): return (out_gate.astype(jnp.float32) * total).astype(jnp.bfloat16)  1.89 us

profile of v8, /device:TPU:0, one launch (start us, length us, event | category | flops | bytes accessed | tf_op | source)
XLA Modules:
  0.0 37.6 jit_solution(2534755852306837398)
XLA Ops:
  0.0 0.0 copy-start.1
  0.0 0.0 copy-start
  0.0 0.0 copy-start.3
  0.0 0.0 copy-start.2
  0.0 35.6 %shard_map.55 = f32[256,512]{1,0:T(8,128)} custom-call(bf16[256,512]{1,0:T(8,128)(2,1)} %in_gate_hbm.1, bf16[256,512]{1,0:T(8,128)(2,1)} %values_hbm.1, bf16[256,512]{1,0:T(8,128)(2,1)} %taps_hbm.1), custom_call_target="tpu_custom_call" | custom-call | tf_op jit(solution)/shard_map/pallas_call | solution.py:318
  35.6 0.0 copy-done.1
  35.6 0.0 copy-done
  35.6 0.0 copy-done.3
  35.7 0.0 copy-done.2
  35.7 1.9 %multiply_convert_fusion = bf16[256,512]{1,0:T(8,128)(2,1)} fusion(f32[256,512]{1,0:T(8,128)} %shard_map.55, bf16[256,512]{1,0:T(8,128)(2,1)S(1)} %copy-done.1, bf16[256,512]{1,0:T(8,128)(2,1)S(1)} %copy-done, bf16[256,512]{1,0:T(8,128)(2,1)S(1)} %copy-done.2, f32[512]{0:T(512)S(1)} %copy-done.3), kind=kLoop, calls=%fused_computation | loop fusion | flops 1048576 | bytes 1574912 | tf_op jit(solution)/shard_map/convert_element_type | solution.py:351
Async XLA Ops:
  0.0 35.6 %copy-start.1 = (bf16[256,512]{1,0:T(8,128)(2,1)S(1)}, bf16[256,512]{1,0:T(8,128)(2,1)}, u32[]{:S(2)}) copy-start(bf16[256,512]{1,0:T(8,128)(2,1)} %values_hbm.1) | copy-start | bytes 786436
  0.0 35.6 %copy-start = (bf16[256,512]{1,0:T(8,128)(2,1)S(1)}, bf16[256,512]{1,0:T(8,128)(2,1)}, u32[]{:S(2)}) copy-start(bf16[256,512]{1,0:T(8,128)(2,1)} %in_gate_hbm.1) | copy-start | bytes 786436
  0.0 35.6 %copy-start.3 = (f32[512]{0:T(512)S(1)}, f32[512]{0:T(512)}, u32[]{:S(2)}) copy-start(f32[512]{0:T(512)} %param.9) | copy-start | bytes 6148
  0.0 35.7 %copy-start.2 = (bf16[256,512]{1,0:T(8,128)(2,1)S(1)}, bf16[256,512]{1,0:T(8,128)(2,1)}, u32[]{:S(2)}) copy-start(bf16[256,512]{1,0:T(8,128)(2,1)} %param.7) | copy-start | bytes 786436
